TPU v7x, 32 devices: a whole 2x2x4 slice. The times are simulated.
32 devices in a mesh: parts: 2 (over x), ctx: 8 (over z, y), head: 2 (over core).
Axes of the slice: x: 2, y: 2, z: 4, core: 2. Of those that a mesh axis runs over, the one named last changes fastest.
Arguments:
- channels: bfloat16 [2048, 2048], P(('parts', 'ctx'), 'head'), parts along dimension 0, may hold values from -6 to 6
- gate_channels: bfloat16 [2048, 2048], P(('parts', 'ctx'), 'head'), parts along dimension 0, may hold values from -6 to 6
- bmat: bfloat16 [2048, 512], P(('parts', 'ctx'), 'head'), parts along dimension 0, may hold values from -4 to 4
- cmat: bfloat16 [2048, 512], P(('parts', 'ctx'), 'head'), parts along dimension 0, may hold values from -4 to 4
- dt: float32 [2048, 32], P(('parts', 'ctx'), 'head'), parts along dimension 0, may hold values from 0.1 to 40
- rates: float32 [32], P('head'), may hold values from 0.00029296876 to 0.03
- skip: float32 [32], P('head'), may hold values from 0.5 to 2
- norm_gain: float32 [2048], P('head'), may hold values from 0.25 to 1.75
- docs: int32 [2048], P(('parts', 'ctx')), parts along dimension 0, may hold values from 0 to 3, never falling along the last dimension, each value on 1 to 512 neighbouring positions
- w_out: bfloat16 [2048, 2688], P('head', 'ctx'), may hold values from -0.125 to 0.125
- residual: bfloat16 [2048, 2688], P(('parts', 'ctx', 'head')), parts along dimension 0, may hold values from -6 to 6
- moe_gain: float32 [2688], replicated, may hold values from 0.25 to 1.75
- experts: int32 [2048, 6], P(('parts', 'ctx', 'head')), parts along dimension 0, may hold values from 0 to 15, all different within a row; in each aligned block of 64 rows (0 to 63, 64 to 127, ...) at most 36 rows name the same one
- gates: float32 [2048, 6], P(('parts', 'ctx', 'head')), parts along dimension 0, may hold values from 0.05 to 0.5
- w_up: bfloat16 [16, 2688, 928], P(('ctx', 'head')), may hold values from -0.125 to 0.125
- w_down: bfloat16 [16, 928, 2688], P(('ctx', 'head')), may hold values from -0.1875 to 0.1875
Outputs:
- layer_out: bfloat16 [2048, 2688], P(('parts', 'ctx', 'head')), parts along dimension 0
There are 2 independent parts, one for each index of `parts`. A program takes and returns all parts, laid end to end along the dimension named above; an argument that names none is the same for every part. Nothing has to cross between parts.
Inputs may be any that keep to these rules, and one draw needn't show every extreme that they name: Each row names 6 different experts; in each aligned block of 64 rows (the rows of one device) no expert is named by more than 36 rows. `docs`: ids never fall along the tokens; a document starts where the id changes and holds at most half of the 1024 tokens.
All inputs are finite; a program needn't handle non-finite values.
Results may differ from a plain program's by a relative error of at most 0.013.
Values may be sent and summed in bfloat16 or wider, within the bound.
A program may use at most 128 MiB of HBM per device.

v0:
```python
import jax
import jax.numpy as jnp
from jax import lax
from jax.sharding import PartitionSpec as P

HEADS = 32
HEAD_DIM = 64
GROUPS = 4
STATE = 128


EPS = 1e-05


def entering(array, axis, combine, identity):
    size, place = (lax.axis_size(axis), lax.axis_index(axis))
    everything = jax.tree.map(lambda part: lax.all_gather(part, axis), array)
    start = jax.tree.map(
        lambda part, zero: jnp.broadcast_to(jnp.asarray(zero, part.dtype), part.shape),
        array,
        identity,
    )

    def lap(k, before):
        reached = k < place
        new = combine(before, jax.tree.map(lambda part: part[k], everything))
        return jax.tree.map(lambda a, b: jnp.where(reached, a, b), new, before)

    return lax.fori_loop(0, size, lap, start)


def silu(value):
    return value / (1.0 + jnp.exp(-value))


def combine_states(earlier, later):
    first_a, last_a, decay_a, state_a = earlier
    first_b, last_b, decay_b, state_b = later
    linked = ((last_a == first_b) | (last_a < 0) | (first_b < 0)).astype(jnp.float32)
    carried = decay_b * linked
    decay = carried * decay_a
    state = state_b + carried[:, None, None] * state_a
    first = jnp.where(first_a < 0, first_b, first_a)
    last = jnp.where(last_b < 0, last_a, last_b)
    return (first, last, decay, state)


def group_terms(inputs, causal, ending):
    x_group, b_group, c_group, log_group, dt_group = inputs
    scores = jnp.dot(c_group, b_group.T, preferred_element_type=jnp.float32)
    gap = jnp.where(causal[:, :, None], log_group[:, None, :] - log_group[None, :, :], -jnp.inf)
    weight = jnp.exp(gap) * scores[:, :, None] * dt_group[None, :, :]
    inner = jnp.einsum("tsh,shp->thp", weight, x_group, precision=lax.Precision.HIGHEST)
    tail = jnp.exp(log_group[-1][None, :] - log_group) * ending[:, None] * dt_group
    end_state = jnp.einsum(
        "sh,shp,sn->hpn",
        tail,
        x_group,
        b_group.astype(jnp.float32),
        precision=lax.Precision.HIGHEST,
    )
    return (inner, end_state)


def expert_rows(received, up_weight, down_weight):
    sources, items, width = received.shape
    rows = received.reshape(sources * items, width)
    up = jnp.dot(rows, up_weight, preferred_element_type=jnp.float32)
    act = jnp.square(jnp.maximum(up, 0.0)).astype(jnp.bfloat16)
    result = jnp.dot(act, down_weight, preferred_element_type=jnp.float32).astype(jnp.bfloat16)
    return result.reshape(sources, items, width)


def local(
    channels,
    gate_channels,
    bmat,
    cmat,
    dt,
    rates,
    skip,
    norm_gain,
    docs,
    w_out,
    residual,
    moe_gain,
    experts,
    gates,
    w_up,
    w_down,
):
    length = channels.shape[0]
    heads = dt.shape[1]
    groups = bmat.shape[1] // STATE
    per_group = heads // groups
    logs = jnp.cumsum(-rates[None, :] * dt, axis=0)
    x_wide = channels.astype(jnp.float32).reshape(length, groups, per_group, HEAD_DIM)
    b_split = bmat.reshape(length, groups, STATE)
    c_split = cmat.reshape(length, groups, STATE)
    position = jnp.arange(length, dtype=jnp.int32)
    causal = (docs[:, None] == docs[None, :]) & (position[:, None] >= position[None, :])
    ending = (docs == docs[length - 1]).astype(jnp.float32)
    opening = (docs == docs[0]).astype(jnp.float32)
    stacked = (
        x_wide.transpose(1, 0, 2, 3),
        b_split.transpose(1, 0, 2),
        c_split.transpose(1, 0, 2),
        logs.reshape(length, groups, per_group).transpose(1, 0, 2),
        dt.reshape(length, groups, per_group).transpose(1, 0, 2),
    )
    inner, end_state = lax.map(lambda item: group_terms(item, causal, ending), stacked)
    end_state = end_state.reshape(heads, HEAD_DIM, STATE)
    whole_decay = jnp.exp(logs[length - 1]) * (docs[0] == docs[length - 1]).astype(jnp.float32)
    element = (docs[:1], docs[length - 1 :], whole_decay, end_state)
    identity = (
        jnp.full((1,), -1, jnp.int32),
        jnp.full((1,), -1, jnp.int32),
        jnp.ones((heads,), jnp.float32),
        jnp.zeros_like(end_state),
    )
    _, prior_last, _, incoming = entering(element, "ctx", combine_states, identity)
    linked = (prior_last == docs[:1]).astype(jnp.float32)
    reach = jnp.exp(logs) * opening[:, None] * linked
    outer = jnp.einsum(
        "tgn,ghpn->tghp",
        c_split.astype(jnp.float32),
        incoming.reshape(groups, per_group, HEAD_DIM, STATE),
        precision=lax.Precision.HIGHEST,
    )
    outer = outer * reach.reshape(length, groups, per_group)[:, :, :, None]
    inner = inner.transpose(1, 0, 2, 3)
    scan = (inner + outer).reshape(length, heads, HEAD_DIM) + skip[None, :, None] * x_wide.reshape(
        length, heads, HEAD_DIM
    )
    scan = scan.reshape(length, heads * HEAD_DIM)
    gated = scan * silu(gate_channels.astype(jnp.float32))
    grouped = gated.reshape(length, -1, HEADS * HEAD_DIM // GROUPS)
    grouped = grouped / jnp.sqrt(jnp.mean(grouped * grouped, axis=2, keepdims=True) + EPS)
    normed_scan = (grouped.reshape(length, -1) * norm_gain).astype(jnp.bfloat16)
    partial_value = jnp.dot(
        normed_scan,
        lax.all_gather(w_out, "ctx", axis=1, tiled=True),
        preferred_element_type=jnp.float32,
    )
    mamba_out = lax.psum_scatter(
        partial_value.astype(jnp.bfloat16), "head", scatter_dimension=0, tiled=True
    ).astype(jnp.float32)
    hidden = (residual.astype(jnp.float32) + mamba_out).astype(jnp.bfloat16)
    widened = hidden.astype(jnp.float32)
    moe_in = (
        widened / jnp.sqrt(jnp.mean(widened * widened, axis=1, keepdims=True) + EPS) * moe_gain
    ).astype(jnp.bfloat16)
    rows_dev = moe_in.shape[0]
    top = experts.shape[1]
    width = moe_in.shape[1]
    ctx_count = lax.axis_size("ctx")
    head_count = lax.axis_size("head")
    experts_all = ctx_count * head_count
    capacity = min(rows_dev, max(4, 3 * rows_dev * top // (2 * experts_all)))
    picks = experts.reshape(-1)
    pick_index = jnp.arange(picks.shape[0], dtype=jnp.int32)
    earlier = (picks[:, None] == picks[None, :]) & (pick_index[None, :] < pick_index[:, None])
    slot = jnp.sum(earlier.astype(jnp.int32), axis=1)
    target = (picks * capacity + slot).reshape(rows_dev, top)
    places = jnp.arange(experts_all * capacity, dtype=jnp.int32)
    routing = jnp.any(target[None, :, :] == places[:, None, None], axis=2).astype(jnp.bfloat16)
    outgoing = jnp.dot(routing, moe_in, preferred_element_type=jnp.float32).astype(jnp.bfloat16)
    outgoing = outgoing.reshape(experts_all, capacity, width)
    up_weight = w_up[0]
    down_weight = w_down[0]
    results = expert_rows(
        lax.all_to_all(outgoing, ("ctx", "head"), split_axis=0, concat_axis=0, tiled=True),
        up_weight,
        down_weight,
    )
    returned = lax.all_to_all(results, ("ctx", "head"), split_axis=0, concat_axis=0, tiled=True)
    flat_back = returned.reshape(experts_all * capacity, width)
    chosen = flat_back[target].astype(jnp.float32)
    mixture = jnp.sum(chosen * gates[:, :, None], axis=1)
    return (widened + mixture).astype(jnp.bfloat16)


def solution(mesh):
    return jax.shard_map(
        local,
        mesh=mesh,
        in_specs=(
            P(("parts", "ctx"), "head"),
            P(("parts", "ctx"), "head"),
            P(("parts", "ctx"), "head"),
            P(("parts", "ctx"), "head"),
            P(("parts", "ctx"), "head"),
            P("head"),
            P("head"),
            P("head"),
            P(("parts", "ctx")),
            P("head", "ctx"),
            P(("parts", "ctx", "head"), None),
            P(),
            P(("parts", "ctx", "head"), None),
            P(("parts", "ctx", "head"), None),
            P(("ctx", "head"), None, None),
            P(("ctx", "head"), None, None),
        ),
        out_specs=P(("parts", "ctx", "head"), None),
        check_vma=False,
    )
```

profile of v0, /device:TPU:13, one launch (start us, length us, event | category | flops | bytes accessed | tf_op | source)
XLA Modules:
  0.0 411.6 jit_solution(10175892320558822707)
XLA Ops:
  6.5 0.7 neg.7
  7.2 0.8 broadcast_multiply_fusion
  8.3 1.0 copy.94
  9.3 1.1 copy.91
  10.4 1.0 copy.95
  11.3 1.3 dynamic-slice
  12.6 1.9 fusion.64
  14.5 1.8 compare_convert_fusion
  16.2 6.9 %while.29 = (s32[]{:T(128)}, f32[2,128,8,64]{1,3,2,0:T(8,128)S(1)}, f32[2,8,64,128]{3,2,1,0:T(8,128)S(1)}, f32[2,128,8,64]{1,3,2,0:T(8,128)S(1)}, f32[2,128,8]{1...) while((s32[]{:T(128)}, f32[2,128,8,64]{1,3,2,0:T(8,128)S(1)}, ...), condition=%wide.region_2.3_spmd.clone, body=%wide.region_1.2_spmd.clone.sunk | while | flops 206162944 | bytes 1364697 | solution.py:111
  16.4 0.8 multiply_multiply_fusion.2
  17.4 0.8 fusion.91
  18.2 1.2 fusion.92
  19.4 0.3 fusion.93
  19.9 0.8 multiply_multiply_fusion.2
  20.9 0.8 fusion.91
  21.7 1.2 fusion.92
  22.9 0.3 fusion.93
  23.2 0.8 copy-done.4
  24.0 0.7 all-gather.8.cloned.1.call-update
  24.8 1.4 slice_dynamic-update-slice_fusion
  26.2 7.9 %all-reduce.2 = (s32[8]{0:T(128)S(1)}, s32[8]{0:T(128)S(1)}) all-reduce(s32[8]{0:T(128)S(1)} %get-tuple-element.359, s32[8]{0:T(128)S(1)} %slice_dynamic-update-slice_fusion), channel_id=2, replica_groups=mesh['parts'=2,'ctx'=8,'head'=2] {'ctx'}, use_global_device_ids=true, to_apply=%add | all-reduce | flops 16 | bytes 128
  35.3 12.0 %all-gather.2 = f32[8,1,16]{2,1,0:T(1,128)S(1)} all-gather(f32[1,1,16]{2,1,0:T(1,128)S(1)} %fusion.61), channel_id=1, replica_groups=mesh['parts'=2,'ctx'=8,'head'=2] {'ctx'}, dimensions={0}, use_global_device_ids=true | all-gather | bytes 576 | tf_op jit(solution)/shard_map/all_gather | solution.py:17
  47.3 48.8 %all-gather.6.cloned.1.call-done = f32[8,16,64,128]{3,2,1,0:T(8,128)} async-done(((f32[1,16,64,128]{3,2,1,0:T(8,128)}), f32[8,16,64,128]{3,2,1,0:T(8,128)}) %all-gather.6.cloned.1.call-update) | async-done | bytes 4194320 | tf_op jit(solution)/shard_map/all_gather | solution.py:17
  96.1 35.5 %while.30 = (s32[]{:T(128)}, s32[1]{0:T(128)}, f32[16,64,128]{2,1,0:T(8,128)S(1)}, s32[]{:T(128)}, s32[8,1]{0,1:T(1,128)S(1)}, /*index=5*/f32[8,16,64,128]{3,2,1...) while((s32[]{:T(128)}, s32[1]{0:T(128)}, ...), condition=%wide.region_4.5_spmd.clone, body=%wide.region_3.4_spmd.clone.sunk | while | flops 524317 | bytes 1573290 | solution.py:29
  96.1 0.7 constant_dynamic-slice_fusion.7
  97.9 1.2 fusion.95
  100.5 0.7 constant_dynamic-slice_fusion.7
  102.4 1.2 fusion.95
  104.9 0.7 constant_dynamic-slice_fusion.7
  106.8 1.2 fusion.95
  109.4 0.7 constant_dynamic-slice_fusion.7
  111.3 1.2 fusion.95
  113.9 0.7 constant_dynamic-slice_fusion.7
  115.7 1.2 fusion.95
  118.3 0.7 constant_dynamic-slice_fusion.7
  120.1 1.2 fusion.95
  122.7 0.7 constant_dynamic-slice_fusion.7
  124.6 1.2 fusion.95
  127.2 0.7 constant_dynamic-slice_fusion.7
  129.0 1.2 fusion.95
  132.2 0.4 fusion.44
  132.8 0.2 fusion.63
  133.0 0.4 mul.211
  133.4 0.2 reduce_sum.38
  134.0 51.5 %all-gather.8.cloned.1.call-done = bf16[1024,2688]{0,1:T(8,128)(2,1)} async-done(((bf16[1024,336]{0,1:T(8,128)(2,1)}), bf16[1024,2688]{0,1:T(8,128)(2,1)}) %all-gather.8.cloned.1.call-update) | async-done | bytes 5505040 | tf_op jit(solution)/shard_map/all_gather | solution.py:142
  185.5 5.4 %convolution_convert_fusion.1 = bf16[128,2688]{1,0:T(8,128)(2,1)} fusion(bf16[1024,2688]{0,1:T(8,128)(2,1)} %all-gather.8.cloned.1.call-done, f32[128,1024]{1,0:T(8,128)S(1)} %bitcast.145, f32[1024]{0:T(1024)S(1)} %copy-done.10, bf16[128,1024]{1,0:T(8,128)(2,1)S(1)} %copy-done.5, f32[128,1024]{1,0:T(8,128)S(1)} %copy.99, f32[1024]{0:T(1024)S(1)} %mul.206, ...), kind=kOutput, calls=%fused_computation.53 | convolution fusion | flops 706428928 | bytes 7774208 | tf_op jit(solution)/shard_map/dot_general | solution.py:140
  191.2 0.2 convert_reduce_fusion
  191.7 0.2 fusion.45
  191.9 9.4 %reduce-scatter.2.cloned.1.call-done = bf16[64,2688]{1,0:T(8,128)(2,1)} async-done(((bf16[128,2688]{1,0:T(8,128)(2,1)}), bf16[64,2688]{1,0:T(8,128)(2,1)}) %reduce-scatter.2.cloned.1.call-update) | async-done | bytes 344080 | tf_op jit(solution)/shard_map/reduce_scatter | solution.py:145
  201.3 1.2 fusion.46
  202.5 2.0 convolution_convert_fusion
  204.5 2.5 reshape.115
  207.0 82.0 %all_to_all.10 = bf16[16,36,2688]{2,1,0:T(8,128)(2,1)S(1)} all-to-all(bf16[16,36,2688]{2,1,0:T(8,128)(2,1)} %reshape.115), channel_id=1, replica_groups=mesh['parts'=2,'ctx'=8,'head'=2] {'ctx','head'}, dimensions={0} | all-to-all | bytes 6193152 | tf_op jit(solution)/shard_map/all_to_all | solution.py:172
  289.0 2.4 reshape.116
  291.3 6.9 %multiply_convert_fusion = bf16[576,928]{1,0:T(8,128)(2,1)S(1)} fusion(bf16[576,2688]{1,0:T(8,128)(2,1)} %reshape.116, bf16[1,2688,928]{1,2,0:T(8,128)(2,1)} %param.34), kind=kOutput, calls=%fused_computation.54 | convolution fusion | flops 2875226112 | bytes 9154560 | tf_op jit(solution)/shard_map/dot_general | solution.py:68
  298.2 6.2 %fusion.38 = bf16[576,2688]{1,0:T(8,128)(2,1)S(1)} fusion(bf16[576,928]{1,0:T(8,128)(2,1)S(1)} %multiply_convert_fusion, bf16[1,928,2688]{2,1,0:T(8,128)(2,1)} %param.35), kind=kOutput, calls=%fused_computation.51 | convolution fusion | flops 2875170816 | bytes 9154560 | tf_op jit(solution)/shard_map/dot_general | solution.py:70
  304.4 2.5 reshape.117
  306.9 5.4 %all-to-all-start.1 = ((bf16[16,36,2688]{2,1,0:T(8,128)(2,1)}), bf16[16,36,2688]{2,1,0:T(8,128)(2,1)}, u32[]{:S(2)}, u32[]{:S(2)}) async-start(bf16[16,36,2688]{2,1,0:T(8,128)(2,1)} %reshape.117), calls=%async_computation.2 | async-start | bytes 6881280 | tf_op jit(solution)/shard_map/all_to_all | solution.py:176
  312.7 76.0 %all-to-all-done.1 = bf16[16,36,2688]{2,1,0:T(8,128)(2,1)} async-done(((bf16[16,36,2688]{2,1,0:T(8,128)(2,1)}), bf16[16,36,2688]{2,1,0:T(8,128)(2,1)}, u32[]{:S(2)}, u32[]{:S(2)}) %all-to-all-start.1) | async-done | bytes 3096608 | tf_op jit(solution)/shard_map/all_to_all | solution.py:176
  388.7 3.0 reshape.118
  391.6 3.4 gather_fusion
  395.1 4.5 %reshape.133 = f32[64,6,2688]{2,1,0:T(8,128)} reshape(bf16[384,2688]{1,0:T(8,128)(2,1)} %gather_fusion) | data formatting | bytes 6193152 | tf_op jit(solution)/shard_map/convert_element_type | solution.py:178
  399.6 4.6 %multiply_reduce_fusion = f32[64,2688]{1,0:T(8,128)S(1)} fusion(f32[64,6,2688]{2,1,0:T(8,128)} %reshape.133, f32[64,6]{1,0:T(8,128)S(1)} %copy.105), kind=kLoop, calls=%fused_computation.46 | loop fusion | flops 1892352 | bytes 4818432 | tf_op jit(solution)/shard_map/reduce_sum | solution.py:179
  404.2 0.8 fusion.49
  (68 shorter events, 2.8 us)
Async XLA Ops:
  6.5 89.5 %all-gather.6.cloned.1.call-start = ((), (), s32[]{:S(2)}) async-start(), calls=%async_computation.3 | async-start | bytes 4718592 | tf_op jit(solution)/shard_map/all_gather | solution.py:17
  16.2 18.9 %copy-start.9 = (f32[16]{0:T(128)S(1)}, f32[16]{0:T(128)}, u32[]{:S(2)}) copy-start(f32[16]{0:T(128)} %param.26) | copy-start | bytes 196
  23.2 0.8 copy-start.4
  24.0 161.5 %all-gather.8.cloned.1.call-start = ((), (), s32[]{:S(2)}) async-start(), calls=%async_computation.4 | async-start | bytes 6193152 | tf_op jit(solution)/shard_map/all_gather | solution.py:142
  24.7 176.5 %reduce-scatter.2.cloned.1.call-start = ((), (), s32[]{:S(2)}) async-start(), calls=%async_computation.5 | async-start | bytes 1032192 | tf_op jit(solution)/shard_map/reduce_scatter | solution.py:145
  96.1 36.7 %copy-start.3 = (bf16[128,1024]{1,0:T(8,128)(2,1)S(1)}, bf16[128,1024]{1,0:T(8,128)(2,1)}, u32[]{:S(2)}) copy-start(bf16[128,1024]{1,0:T(8,128)(2,1)} %param.20) | copy-start | bytes 786436
  96.1 36.7 %copy-start.5 = (bf16[128,1024]{1,0:T(8,128)(2,1)S(1)}, bf16[128,1024]{1,0:T(8,128)(2,1)}, u32[]{:S(2)}) copy-start(bf16[128,1024]{1,0:T(8,128)(2,1)} %param.21) | copy-start | bytes 786436
  132.2 53.4 %copy-start.10 = (f32[1024]{0:T(1024)S(1)}, f32[1024]{0:T(1024)}, u32[]{:S(2)}) copy-start(f32[1024]{0:T(1024)} %param.27) | copy-start | bytes 12292
  185.5 5.4 %copy-start.6 = (s32[64,6]{0,1:T(8,128)S(1)}, s32[64,6]{0,1:T(8,128)}, u32[]{:S(2)}) copy-start(s32[64,6]{0,1:T(8,128)} %param.32) | copy-start | bytes 4612
  185.5 15.7 %copy-start = (bf16[64,2688]{1,0:T(8,128)(2,1)S(1)}, bf16[64,2688]{1,0:T(8,128)(2,1)}, u32[]{:S(2)}) copy-start(bf16[64,2688]{1,0:T(8,128)(2,1)} %param.30) | copy-start | bytes 1032196
  185.5 17.0 %copy-start.7 = (f32[2688]{0:T(1024)S(1)}, f32[2688]{0:T(1024)}, u32[]{:S(2)}) copy-start(f32[2688]{0:T(1024)} %param.31) | copy-start | bytes 32260
  306.9 5.7 %copy-start.8 = (f32[64,6]{0,1:T(8,128)S(1)}, f32[64,6]{0,1:T(8,128)}, u32[]{:S(2)}) copy-start(f32[64,6]{0,1:T(8,128)} %param.33) | copy-start | bytes 4612
  306.9 81.8 %all-to-all-start.1 = ((bf16[16,36,2688]{2,1,0:T(8,128)(2,1)}), bf16[16,36,2688]{2,1,0:T(8,128)(2,1)}, u32[]{:S(2)}, u32[]{:S(2)}) async-start(bf16[16,36,2688]{2,1,0:T(8,128)(2,1)} %reshape.117), calls=%async_computation.2 | async-start | bytes 6881280 | tf_op jit(solution)/shard_map/all_to_all | solution.py:176
  399.6 4.6 %copy-start.1 = (bf16[64,2688]{1,0:T(8,128)(2,1)S(1)}, bf16[64,2688]{1,0:T(8,128)(2,1)}, u32[]{:S(2)}) copy-start(bf16[64,2688]{1,0:T(8,128)(2,1)} %param.30) | copy-start | bytes 1032196
  399.6 4.6 %copy-start.2 = (bf16[64,2688]{1,0:T(8,128)(2,1)S(1)}, bf16[64,2688]{1,0:T(8,128)(2,1)}, u32[]{:S(2)}) copy-start(bf16[64,2688]{1,0:T(8,128)(2,1)} %reduce-scatter.2.cloned.1.call-done) | copy-start | bytes 1032196
Sparse Core Ops, SparseCore 0:
  24.1 71.9 all-gather.5
  98.3 87.2 all-gather.7
  191.1 10.1 reduce-scatter.1
where the time goes:
time: 413 us; the launch traced here: 412 us
  waiting for transfers between devices  186 us (45%)
  blocking collectives  102 us (25%)
  local copies, waits for them, and re-layouts  34.4 us (8%)
  matrix products  24.1 us (6%)
  other arithmetic  23.6 us (6%)
  loops' own time  20.7 us (5%)
  between operations  15.1 us (4%)
  starting transfers between devices  5.51 us (1%)
    all_to_all x1, blocking collectives, local(): lax.all_to_all(outgoing, ('ctx', 'head'), split_axis=0, concat_axis=0, ti...  82 us
    all_to_all x1, waiting for transfers between devices, local(): lax.all_to_all(results, ('ctx', 'head'), split_axis=0, concat_axis=0, til...  76 us
    all_gather x1, waiting for transfers between devices, local(): lax.all_gather(w_out, 'ctx', axis=1, tiled=True)  51.5 us
    all_gather x1, waiting for transfers between devices, entering(): everything = jax.tree.map(lambda part: lax.all_gather(part, axis), array)  48.8 us
    another operation x1, loops' own time, entering(): return lax.fori_loop(0, size, lap, start)  20.6 us
    all_gather x1, blocking collectives, entering(): everything = jax.tree.map(lambda part: lax.all_gather(part, axis), array)  12 us
    select_n x8, other arithmetic, lap(): return jax.tree.map(lambda a, b: jnp.where(reached, a, b), new, before)  9.44 us
    reduce_scatter x1, waiting for transfers between devices, local(): lax.psum_scatter(partial_value.astype(jnp.bfloat16), 'head', scatter_dime...  9.37 us
  transfers between devices with their start and end apart: 4, of which 4 were waited for; matrix products, arithmetic and copies ran while one was open for 5% of the time, Pallas kernels for 0%

commit v1 on v0

--- a/solution.py
+++ b/solution.py
@@ -1,6 +1,10 @@
+import functools
+
 import jax
 import jax.numpy as jnp
 from jax import lax
+from jax.experimental import pallas as pl
+from jax.experimental.pallas import tpu as pltpu
 from jax.sharding import PartitionSpec as P
 
 HEADS = 32
@@ -69,6 +73,294 @@
     act = jnp.square(jnp.maximum(up, 0.0)).astype(jnp.bfloat16)
     result = jnp.dot(act, down_weight, preferred_element_type=jnp.float32).astype(jnp.bfloat16)
     return result.reshape(sources, items, width)
+
+
+MESH = pl.DeviceIdType.MESH
+LANES = 128
+
+
+def ring_place(index, size):
+    half, odd = index // 2, index % 2
+    return (1 - odd) * half + odd * (size - 1 - half)
+
+
+def ring_index(place, size):
+    back = place // (size // 2)
+    return (1 - back) * (2 * place) + back * (2 * (size - 1 - place) + 1)
+
+
+def moe_kernel(
+    n,
+    heads,
+    hidden_ref,
+    gain_ref,
+    gate_ref,
+    up_hbm,
+    down_hbm,
+    out_ref,
+    rows_ref,
+    part_ref,
+    lent_ref,
+    borrowed_ref,
+    sums_ref,
+    act_ref,
+    up_ref,
+    down_ref,
+    weight_sem,
+    ag_send,
+    ag_recv,
+    sib_send,
+    sib_recv,
+    lend_send,
+    lend_recv,
+    rs_send,
+    rs_recv,
+):
+    rows, width = hidden_ref.shape
+    both = 2 * rows
+    inner = up_ref.shape[1]
+    half = n // 2
+    cut = rows // 2
+    place = ring_place(lax.axis_index("ctx"), n)
+    head = lax.axis_index("head")
+    mine = lax.axis_index("ctx") * heads + head
+    after = {"ctx": ring_index((place + 1) % n, n)}
+    before = {"ctx": ring_index((place + n - 1) % n, n)}
+    sibling = {"head": 1 - head}
+
+    up_copy = pltpu.make_async_copy(up_hbm.at[0], up_ref, weight_sem.at[0])
+    down_copy = pltpu.make_async_copy(down_hbm.at[0], down_ref, weight_sem.at[1])
+    up_copy.start()
+    down_copy.start()
+
+    barrier = pltpu.get_barrier_semaphore()
+    for device in (after, before, sibling):
+        pl.semaphore_signal(barrier, inc=1, device_id=device, device_id_type=MESH)
+
+    def slot(s):
+        if s == 0:
+            return 0
+        if s == half:
+            return 1
+        return 2 * s if s < half else 2 * (n - s) + 1
+
+    def send(source, target, send_sem, recv_sem, device):
+        copy = pltpu.make_async_remote_copy(
+            src_ref=source,
+            dst_ref=target,
+            send_sem=send_sem,
+            recv_sem=recv_sem,
+            device_id=device,
+            device_id_type=MESH,
+        )
+        copy.start()
+        return copy
+
+    hidden = hidden_ref[...].astype(jnp.float32)
+    scale = jnp.sqrt(jnp.mean(hidden * hidden, axis=1, keepdims=True) + EPS)
+    rows_ref[pl.ds(0, rows), pl.ds(0, width)] = (hidden / scale * gain_ref[...]).astype(jnp.bfloat16)
+    gate = gate_ref[...]
+    high = gate.astype(jnp.bfloat16).astype(jnp.float32)
+    lane = lax.broadcasted_iota(jnp.int32, gate.shape, 1)
+    rows_ref[pl.ds(0, rows), pl.ds(width, LANES)] = jnp.where(lane < LANES // 2, high, gate - high).astype(jnp.bfloat16)
+
+    pl.semaphore_wait(barrier, 3)
+
+    def hop(k):
+        lo, size_up, size_down = 0, rows, rows
+        start_up, start_down = 0, 0
+        if k == half:
+            size_up, size_down, start_down = cut, rows - cut, cut
+        source_up = rows_ref.at[pl.ds(slot(k - 1) * both + start_up, size_up)]
+        target_up = rows_ref.at[pl.ds(slot(k) * both + start_up, size_up)]
+        source_down = rows_ref.at[pl.ds(slot((n - k + 1) % n) * both + start_down, size_down)]
+        target_down = rows_ref.at[pl.ds(slot(n - k) * both + start_down, size_down)]
+        return (
+            send(source_up, target_up, ag_send.at[0, k - 1], ag_recv.at[0, k - 1], after),
+            send(source_down, target_down, ag_send.at[1, k - 1], ag_recv.at[1, k - 1], before),
+        )
+
+    def share(s):
+        return send(
+            rows_ref.at[pl.ds(slot(s) * both, rows)],
+            rows_ref.at[pl.ds(slot(s) * both + rows, rows)],
+            sib_send.at[slot(s)],
+            sib_recv.at[slot(s)],
+            sibling,
+        )
+
+    column = lax.broadcasted_iota(jnp.int32, (both, LANES), 1)
+
+    def expert(slots):
+        count = len(slots) * both
+        first = slots[0]
+        block = pl.ds(first * both, count)
+
+        def up(columns):
+            value = jnp.dot(
+                rows_ref[block, pl.ds(0, width)], up_ref[:, columns], preferred_element_type=jnp.float32
+            )
+            value = jnp.maximum(value, 0.0)
+            act_ref[pl.ds(0, count), columns] = (value * value).astype(jnp.bfloat16)
+
+        tile = 2 * LANES
+
+        @pl.loop(0, inner // tile)
+        def _(i):
+            up(pl.ds(pl.multiple_of(i * tile, tile), tile))
+
+        if inner % tile:
+            up(pl.ds(inner // tile * tile, inner % tile))
+
+        weights = []
+        for s in slots:
+            carried = rows_ref[pl.ds(s * both, both), pl.ds(width, LANES)].astype(jnp.float32)
+            chosen = (column == mine) | (column == mine + LANES // 2)
+            weights.append(jnp.sum(jnp.where(chosen, carried, 0.0), axis=1, keepdims=True))
+
+        def down(columns):
+            value = jnp.dot(
+                act_ref[pl.ds(0, count), :], down_ref[:, columns], preferred_element_type=jnp.float32
+            )
+            for i, s in enumerate(slots):
+                own = value[i * both : i * both + rows] * weights[i][:rows]
+                other = value[i * both + rows : (i + 1) * both] * weights[i][rows:]
+                part_ref[s, :, columns] = own.astype(jnp.bfloat16)
+                lent_ref[s, :, columns] = other.astype(jnp.bfloat16)
+
+        wide = width // LANES
+        step = max(d for d in (1, 2, 3, 4) if wide % d == 0) * LANES
+
+        @pl.loop(0, width // step)
+        def _(i):
+            down(pl.ds(pl.multiple_of(i * step, LANES), step))
+
+        return [
+            send(lent_ref.at[s], borrowed_ref.at[s], lend_send.at[s], lend_recv.at[s], sibling) for s in slots
+        ]
+
+    loans = {}
+    started = list(hop(1))
+    arriving = started
+    shares = {0: share(0)}
+    up_copy.wait()
+    down_copy.wait()
+    shares[0].wait_recv()
+    loans[slot(0)] = expert([slot(0)])[0]
+    for k in range(1, half + 1):
+        for copy in arriving:
+            copy.wait_recv()
+        if k < half:
+            arriving = hop(k + 1)
+            started += list(arriving)
+        near = [k, n - k] if k < half else [k]
+        for s in near:
+            shares[s] = share(s)
+        for s in near:
+            shares[s].wait_recv()
+        lent = expert([slot(s) for s in near])
+        for s, copy in zip(near, lent):
+            loans[slot(s)] = copy
+
+    def total(s, inbound):
+        loans[slot(s)].wait_recv()
+        value = part_ref[slot(s)].astype(jnp.float32) + borrowed_ref[slot(s)].astype(jnp.float32)
+        return value
+
+    backs = []
+
+    def give(s, low, high, down, k):
+        piece = pl.ds(low, high - low)
+        if down:
+            nearer = s - 1 if s > 1 else 0
+            return send(
+                part_ref.at[slot(s), piece],
+                sums_ref.at[slot(nearer), piece],
+                rs_send.at[0, k - 1],
+                rs_recv.at[0, k - 1],
+                before,
+            )
+        nearer = s + 1 if s + 1 < n else half
+        return send(
+            part_ref.at[slot(s), piece],
+            sums_ref.at[slot(nearer), piece],
+            rs_send.at[1, k - 1],
+            rs_recv.at[1, k - 1],
+            after,
+        )
+
+    part_ref[slot(half)] = total(half, None).astype(jnp.bfloat16)
+    coming = [give(half, 0, cut, True, half), give(half, cut, rows, False, half)]
+    backs += coming
+    for k in range(half - 1, 0, -1):
+        lower = total(k, None)
+        upper = total(n - k, None)
+        part_ref[slot(k)] = lower.astype(jnp.bfloat16)
+        part_ref[slot(n - k)] = upper.astype(jnp.bfloat16)
+        following = []
+        for way, (s, copy) in enumerate(zip((k, n - k), coming)):
+            copy.wait_recv()
+            piece = pl.ds(0, rows)
+            if k == half - 1:
+                piece = pl.ds(0, cut) if way == 0 else pl.ds(cut, rows - cut)
+            value = part_ref[slot(s), piece].astype(jnp.float32) + sums_ref[slot(s), piece].astype(jnp.float32)
+            part_ref[slot(s), piece] = value.astype(jnp.bfloat16)
+            following.append(give(s, 0, rows, way == 0, k))
+        coming = following
+        backs += coming
+    value = hidden_ref[...].astype(jnp.float32) + total(0, None)
+    for copy in coming:
+        copy.wait_recv()
+    value = value + sums_ref[slot(0)].astype(jnp.float32) + sums_ref[slot(half)].astype(jnp.float32)
+    out_ref[...] = value.astype(jnp.bfloat16)
+    for copy in started + list(shares.values()) + list(loans.values()) + backs:
+        copy.wait_send()
+
+
+def moe_on_ring(hidden, moe_gain, experts, gates, w_up, w_down):
+    n, heads = lax.axis_size("ctx"), lax.axis_size("head")
+    rows, width = hidden.shape
+    inner = w_up.shape[2]
+    lane = jnp.arange(LANES, dtype=jnp.int32) % (LANES // 2)
+    gate = jnp.sum(jnp.where(experts[:, :, None] == lane[None, None, :], gates[:, :, None], 0.0), axis=1)
+    vmem = pl.BlockSpec(memory_space=pltpu.VMEM)
+    anywhere = pl.BlockSpec(memory_space=pl.ANY)
+    pieces = pltpu.VMEM((n, rows, width), jnp.bfloat16)
+    return pl.pallas_call(
+        functools.partial(moe_kernel, n, heads),
+        out_shape=jax.ShapeDtypeStruct((rows, width), jnp.bfloat16),
+        in_specs=[vmem, vmem, vmem, anywhere, anywhere],
+        out_specs=vmem,
+        scratch_shapes=[
+            pltpu.VMEM((n * 2 * rows, width + LANES), jnp.bfloat16),
+            pieces,
+            pieces,
+            pieces,
+            pieces,
+            pltpu.VMEM((4 * rows, inner), jnp.bfloat16),
+            pltpu.VMEM((width, inner), jnp.bfloat16),
+            pltpu.VMEM((inner, width), jnp.bfloat16),
+            pltpu.SemaphoreType.DMA((2,)),
+            pltpu.SemaphoreType.DMA((2, n // 2)),
+            pltpu.SemaphoreType.DMA((2, n // 2)),
+            pltpu.SemaphoreType.DMA((n,)),
+            pltpu.SemaphoreType.DMA((n,)),
+            pltpu.SemaphoreType.DMA((n,)),
+            pltpu.SemaphoreType.DMA((n,)),
+            pltpu.SemaphoreType.DMA((2, n // 2)),
+            pltpu.SemaphoreType.DMA((2, n // 2)),
+        ],
+        compiler_params=pltpu.CompilerParams(
+            collective_id=1, has_side_effects=True, vmem_limit_bytes=56 * 2**20
+        ),
+        cost_estimate=pl.CostEstimate(
+            flops=8 * n * rows * width * inner, bytes_accessed=4 * width * inner, transcendentals=0
+        ),
+    )(hidden, moe_gain.reshape(1, width), gate, w_up, w_down)
+
+
+def ring_fits(n, heads, rows, width):
+    return n % 2 == 0 and n >= 4 and heads == 2 and rows % 32 == 0 and width % LANES == 0 and n * heads <= LANES // 2 and 14 * n * rows * width <= 24 * 2**20
 
 
 def local(
@@ -146,6 +438,8 @@
         partial_value.astype(jnp.bfloat16), "head", scatter_dimension=0, tiled=True
     ).astype(jnp.float32)
     hidden = (residual.astype(jnp.float32) + mamba_out).astype(jnp.bfloat16)
+    if ring_fits(lax.axis_size("ctx"), lax.axis_size("head"), *hidden.shape):
+        return moe_on_ring(hidden, moe_gain, experts, gates, w_up, w_down)
     widened = hidden.astype(jnp.float32)
     moe_in = (
         widened / jnp.sqrt(jnp.mean(widened * widened, axis=1, keepdims=True) + EPS) * moe_gain

time: 413 us -> 293 us (0.71)
  the two profiles are of different devices: /device:TPU:13 before, /device:TPU:0 now
where the time goes in v1:
time: 293 us; the launch traced here: 292 us
  waiting for transfers between devices  95.5 us (33%)
  Pallas kernels  76.1 us (26%)
  blocking collectives  31.1 us (11%)
  local copies, waits for them, and re-layouts  25.4 us (9%)
  loops' own time  19.9 us (7%)
  other arithmetic  19.3 us (7%)
  between operations  15.4 us (5%)
  matrix products  9.04 us (3%)
    pallas_call x1, Pallas kernels, moe_on_ring(): pl.pallas_call(functools.partial(moe_kernel, n, heads), out_shape=jax.Sha...  76.1 us
    all_gather x1, waiting for transfers between devices, local(): lax.all_gather(w_out, 'ctx', axis=1, tiled=True)  53.1 us
    all_gather x1, waiting for transfers between devices, entering(): everything = jax.tree.map(lambda part: lax.all_gather(part, axis), array)  41.6 us
    another operation x1, loops' own time, entering(): return lax.fori_loop(0, size, lap, start)  19.8 us
    all_gather x1, blocking collectives, entering(): everything = jax.tree.map(lambda part: lax.all_gather(part, axis), array)  17.9 us
    unnamed x27, local copies, waits for them, and re-layouts  15.4 us
    unnamed x1, blocking collectives  13.1 us
    select_n x8, other arithmetic, lap(): return jax.tree.map(lambda a, b: jnp.where(reached, a, b), new, before)  9.39 us
  transfers between devices with their start and end apart: 3, of which 2 were waited for; matrix products, arithmetic and copies ran while one was open for 9% of the time, Pallas kernels for 0%

profile of v1, /device:TPU:0, one launch (start us, length us, event | category | flops | bytes accessed | tf_op | source)
XLA Modules:
  0.0 291.7 jit_solution(14421488251475245178)
XLA Ops:
  6.5 0.7 neg.7
  7.2 0.8 broadcast_multiply_fusion
  8.0 0.1 copy.83
  8.1 0.2 reduce_window_sum.11
  8.2 0.1 copy.84
  8.3 1.0 copy.85
  9.3 1.1 copy.82
  10.4 1.0 copy.86
  11.3 1.2 dynamic-slice
  12.6 1.9 fusion.46
  14.5 2.0 compare_convert_fusion
  16.5 6.9 %while.29 = (s32[]{:T(128)}, f32[2,128,8,64]{1,3,2,0:T(8,128)S(1)}, f32[2,8,64,128]{3,2,1,0:T(8,128)S(1)}, f32[2,128,8,64]{1,3,2,0:T(8,128)S(1)}, f32[2,128,8]{1...) while((s32[]{:T(128)}, f32[2,128,8,64]{1,3,2,0:T(8,128)S(1)}, ...), condition=%wide.region_2.3_spmd.clone, body=%wide.region_1.2_spmd.clone.sunk | while | flops 206162944 | bytes 1364697 | solution.py:403
  16.5 0.2 slice_reduce_fusion.2
  16.6 0.8 multiply_multiply_fusion.2
  17.4 0.2 fusion.68
  17.6 0.8 fusion.70
  18.4 1.2 fusion.71
  19.6 0.3 fusion.72
  19.9 0.2 slice_reduce_fusion.2
  20.1 0.8 multiply_multiply_fusion.2
  20.9 0.2 fusion.68
  21.1 0.8 fusion.70
  21.9 1.2 fusion.71
  23.1 0.3 fusion.72
  23.4 0.8 copy-done.1
  24.3 0.7 all-gather.8.cloned.1.call-update
  25.0 1.3 slice_dynamic-update-slice_fusion
  26.3 13.1 %all-reduce.2 = (s32[8]{0:T(128)S(1)}, s32[8]{0:T(128)S(1)}) all-reduce(s32[8]{0:T(128)S(1)} %get-tuple-element.357, s32[8]{0:T(128)S(1)} %slice_dynamic-update-slice_fusion), channel_id=2, replica_groups=mesh['parts'=2,'ctx'=8,'head'=2] {'ctx'}, use_global_device_ids=true, to_apply=%add | all-reduce | flops 16 | bytes 128
  40.9 0.1 mul.177
  40.9 0.1 mul.178
  41.0 17.9 %all-gather.2 = f32[8,1,16]{2,1,0:T(1,128)S(1)} all-gather(f32[1,1,16]{2,1,0:T(1,128)S(1)} %fusion.43), channel_id=1, replica_groups=mesh['parts'=2,'ctx'=8,'head'=2] {'ctx'}, dimensions={0}, use_global_device_ids=true | all-gather | bytes 576 | tf_op jit(solution)/shard_map/all_gather | solution.py:21
  59.0 41.6 %all-gather.6.cloned.1.call-done = f32[8,16,64,128]{3,2,1,0:T(8,128)} async-done(((f32[1,16,64,128]{3,2,1,0:T(8,128)}), f32[8,16,64,128]{3,2,1,0:T(8,128)}) %all-gather.6.cloned.1.call-update) | async-done | bytes 4194320 | tf_op jit(solution)/shard_map/all_gather | solution.py:21
  100.6 34.2 %while.30 = (s32[]{:T(128)}, s32[1]{0:T(128)}, f32[16,64,128]{2,1,0:T(8,128)S(1)}, s32[]{:T(128)}, s32[8,1]{0,1:T(1,128)S(1)}, /*index=5*/f32[8,16,64,128]{3,2,1...) while((s32[]{:T(128)}, s32[1]{0:T(128)}, ...), condition=%wide.region_4.5_spmd.clone, body=%wide.region_3.4_spmd.clone.sunk | while | flops 524317 | bytes 1573290 | solution.py:33
  100.6 0.6 constant_dynamic-slice_fusion.7
  102.5 1.2 fusion.74
  104.9 0.6 constant_dynamic-slice_fusion.7
  106.8 1.2 fusion.74
  109.1 0.6 constant_dynamic-slice_fusion.7
  111.1 1.2 fusion.74
  113.4 0.6 constant_dynamic-slice_fusion.7
  115.3 1.2 fusion.74
  117.7 0.6 constant_dynamic-slice_fusion.7
  119.6 1.2 fusion.74
  122.0 0.6 constant_dynamic-slice_fusion.7
  123.9 1.2 fusion.74
  126.2 0.6 constant_dynamic-slice_fusion.7
  128.2 1.2 fusion.74
  130.5 0.6 constant_dynamic-slice_fusion.7
  132.4 1.2 fusion.74
  135.5 0.4 fusion.35
  135.9 0.2 copy.90
  136.1 0.2 fusion.45
  136.3 0.4 mul.183
  136.8 0.2 reduce_sum.18
  137.1 0.2 div.23
  137.3 0.1 copy.99
  137.4 53.1 %all-gather.8.cloned.1.call-done = bf16[1024,2688]{0,1:T(8,128)(2,1)} async-done(((bf16[1024,336]{0,1:T(8,128)(2,1)}), bf16[1024,2688]{0,1:T(8,128)(2,1)}) %all-gather.8.cloned.1.call-update) | async-done | bytes 5505040 | tf_op jit(solution)/shard_map/all_gather | solution.py:434
  190.5 5.4 %convolution_convert_fusion = bf16[128,2688]{1,0:T(8,128)(2,1)} fusion(bf16[1024,2688]{0,1:T(8,128)(2,1)} %all-gather.8.cloned.1.call-done, f32[128,1024]{1,0:T(8,128)S(1)} %bitcast.132, f32[1024]{0:T(1024)S(1)} %copy-done.8, bf16[128,1024]{1,0:T(8,128)(2,1)S(1)} %copy-done.3, f32[128,1024]{1,0:T(8,128)S(1)} %copy.90, f32[1024]{0:T(1024)S(1)} %mul.178, ...), kind=kOutput, calls=%fused_computation.45 | convolution fusion | flops 706428928 | bytes 7774208 | tf_op jit(solution)/shard_map/dot_general | solution.py:432
  195.9 8.2 %copy.93.up_hbm = bf16[1,2688,928]{2,1,0:T(8,128)(2,1)} copy(bf16[1,2688,928]{1,2,0:T(8,128)(2,1)} %param.34) | data formatting | bytes 9977856 | tf_op args[14]
  204.2 0.6 reshape.96.gain_ref
  204.8 0.8 select_reduce_fusion.gate_ref
  205.6 1.8 add_convert_fusion.hidden_ref
  207.3 76.1 %shard_map.154 = bf16[64,2688]{1,0:T(8,128)(2,1)} custom-call(bf16[64,2688]{1,0:T(8,128)(2,1)} %add_convert_fusion.hidden_ref, f32[1,2688]{1,0:T(1,128)} %reshape.96.gain_ref, f32[64,128]{1,0:T(8,128)} %select_reduce_fusion.gate_ref, bf16[1,2688,928]{2,1,0:T(8,128)(2,1)} %copy.93.up_hbm, bf16[1,928,2688]{2,1,0:T(8,128)(2,1)} %down_hbm.1), custom_call_target="tpu_custom_call" | custom-call | flops 10217324544 | bytes 9977856 | tf_op jit(solution)/shard_map/pallas_call | solution.py:329
  283.5 1.7 copy.128
  (44 shorter events, 0.3 us)
Async XLA Ops:
  6.5 94.1 %all-gather.6.cloned.1.call-start = ((), (), s32[]{:S(2)}) async-start(), calls=%async_computation.1 | async-start | bytes 4718592 | tf_op jit(solution)/shard_map/all_gather | solution.py:21
  9.3 31.6 %copy-start.7 = (f32[16]{0:T(128)S(1)}, f32[16]{0:T(128)}, u32[]{:S(2)}) copy-start(f32[16]{0:T(128)} %param.26) | copy-start | bytes 196
  23.4 0.8 copy-start.1
  24.2 166.3 %all-gather.8.cloned.1.call-start = ((), (), s32[]{:S(2)}) async-start(), calls=%async_computation.2 | async-start | bytes 6193152 | tf_op jit(solution)/shard_map/all_gather | solution.py:434
  25.0 180.6 %reduce-scatter.2.cloned.1.call-start = ((), (), s32[]{:S(2)}) async-start(), calls=%async_computation.3 | async-start | bytes 1032192 | tf_op jit(solution)/shard_map/reduce_scatter | solution.py:437
  40.8 95.3 %copy-start = (bf16[128,1024]{1,0:T(8,128)(2,1)S(1)}, bf16[128,1024]{1,0:T(8,128)(2,1)}, u32[]{:S(2)}) copy-start(bf16[128,1024]{1,0:T(8,128)(2,1)} %param.20) | copy-start | bytes 786436
  40.9 95.3 %copy-start.3 = (bf16[128,1024]{1,0:T(8,128)(2,1)S(1)}, bf16[128,1024]{1,0:T(8,128)(2,1)}, u32[]{:S(2)}) copy-start(bf16[128,1024]{1,0:T(8,128)(2,1)} %param.21) | copy-start | bytes 786436
  134.8 55.7 %copy-start.8 = (f32[1024]{0:T(1024)S(1)}, f32[1024]{0:T(1024)}, u32[]{:S(2)}) copy-start(f32[1024]{0:T(1024)} %param.27) | copy-start | bytes 12292
  195.9 8.3 %copy-start.4 = (f32[2688]{0:T(1024)S(1)}, f32[2688]{0:T(1024)}, u32[]{:S(2)}) copy-start(f32[2688]{0:T(1024)} %param.31) | copy-start | bytes 32260
  195.9 8.9 %copy-start.5 = (f32[64,6]{0,1:T(8,128)S(1)}, f32[64,6]{0,1:T(8,128)}, u32[]{:S(2)}) copy-start(f32[64,6]{0,1:T(8,128)} %param.33) | copy-start | bytes 4612
  195.9 8.9 %copy-start.6 = (s32[64,6]{0,1:T(8,128)S(1)}, s32[64,6]{0,1:T(8,128)}, u32[]{:S(2)}) copy-start(s32[64,6]{0,1:T(8,128)} %param.32) | copy-start | bytes 4612
  195.9 9.7 %copy-start.2 = (bf16[64,2688]{1,0:T(8,128)(2,1)S(1)}, bf16[64,2688]{1,0:T(8,128)(2,1)}, u32[]{:S(2)}) copy-start(bf16[64,2688]{1,0:T(8,128)(2,1)} %param.30) | copy-start | bytes 1032196
Sparse Core Ops, SparseCore 0:
  24.3 76.1 all-gather.5
  102.8 87.7 all-gather.7
  196.0 6.3 reduce-scatter.1

commit v2 on v1

--- a/solution.py
+++ b/solution.py
@@ -89,15 +89,39 @@
     return (1 - back) * (2 * place) + back * (2 * (size - 1 - place) + 1)
 
 
-def moe_kernel(
+def layer_kernel(
     n,
     heads,
-    hidden_ref,
+    x_ref,
+    silu_ref,
+    b_ref,
+    c_ref,
+    dt_ref,
+    rates_ref,
+    skip_ref,
+    norm_ref,
+    docs_col_ref,
+    docs_row_ref,
+    proj_ref,
+    residual_ref,
     gain_ref,
     gate_ref,
     up_hbm,
     down_hbm,
     out_ref,
+    meta_ref,
+    reach_ref,
+    state_ref,
+    scan_ref,
+    incoming_ref,
+    normed_ref,
+    product_ref,
+    product_lent_ref,
+    product_got_ref,
+    block_ref,
+    columns_ref,
+    mamba_ref,
+    hidden_ref,
     rows_ref,
     part_ref,
     lent_ref,
@@ -107,6 +131,16 @@
     up_ref,
     down_ref,
     weight_sem,
+    meta_send,
+    meta_recv,
+    state_send,
+    state_recv,
+    normed_send,
+    normed_recv,
+    product_send,
+    product_recv,
+    block_send,
+    block_recv,
     ag_send,
     ag_recv,
     sib_send,
@@ -116,9 +150,9 @@
     rs_send,
     rs_recv,
 ):
-    rows, width = hidden_ref.shape
+    rows, width = residual_ref.shape
     both = 2 * rows
-    inner = up_ref.shape[1]
+    inner = up_ref.shape[0]
     half = n // 2
     cut = rows // 2
     place = ring_place(lax.axis_index("ctx"), n)
@@ -133,9 +167,11 @@
     up_copy.start()
     down_copy.start()
 
+    me = lax.axis_index("ctx")
     barrier = pltpu.get_barrier_semaphore()
-    for device in (after, before, sibling):
-        pl.semaphore_signal(barrier, inc=1, device_id=device, device_id_type=MESH)
+    for d in range(1, n):
+        pl.semaphore_signal(barrier, inc=1, device_id={"ctx": (me + d) % n}, device_id_type=MESH)
+    pl.semaphore_signal(barrier, inc=1, device_id=sibling, device_id_type=MESH)
 
     def slot(s):
         if s == 0:
@@ -156,29 +192,199 @@
         copy.start()
         return copy
 
-    hidden = hidden_ref[...].astype(jnp.float32)
+    def ring_hop(ref, stride, size, send_sem, recv_sem, k):
+        up_start, up_size, down_start, down_size = 0, size, 0, size
+        if k == half:
+            up_size, down_start, down_size = size // 2, size // 2, size // 2
+        up_from = ref.at[pl.ds(slot(k - 1) * stride + up_start, up_size)]
+        up_to = ref.at[pl.ds(slot(k) * stride + up_start, up_size)]
+        down_from = ref.at[pl.ds(slot((n - k + 1) % n) * stride + down_start, down_size)]
+        down_to = ref.at[pl.ds(slot(n - k) * stride + down_start, down_size)]
+        return [
+            send(up_from, up_to, send_sem.at[0, k - 1], recv_sem.at[0, k - 1], after),
+            send(down_from, down_to, send_sem.at[1, k - 1], recv_sem.at[1, k - 1], before),
+        ]
+
+    def across(a, b):
+        return lax.dot_general(
+            a, b, (((1,), (1,)), ((), ())), precision=lax.Precision.HIGHEST, preferred_element_type=jnp.float32
+        )
+
+    def exact(a, b):
+        return jnp.dot(a, b, precision=lax.Precision.HIGHEST, preferred_element_type=jnp.float32)
+
+    length, channels = x_ref.shape
+    own_heads = dt_ref.shape[0]
+    groups = b_ref.shape[1] // STATE
+    span = channels // groups
+    f32 = jnp.float32
+    pending = []
+
+    at_row = lax.broadcasted_iota(jnp.int32, (length, length), 0)
+    at_column = lax.broadcasted_iota(jnp.int32, (length, length), 1)
+    lower = jnp.where(at_row >= at_column, 1.0, 0.0)
+    identity = jnp.where(at_row == at_column, 1.0, 0.0)
+    dt_heads = dt_ref[...]
+    slow = jnp.concatenate([-rates_ref[...] * dt_heads, jnp.zeros((LANES - own_heads, length), f32)], axis=0)
+    logs = across(lower, slow)
+    logs_heads = across(slow, lower)
+    docs_col, docs_row = docs_col_ref[...], docs_row_ref[...]
+    first, last = docs_row[:, :1], docs_row[:, length - 1 :]
+    lane = lax.broadcasted_iota(jnp.int32, (1, LANES), 1)
+    note = jnp.where(lane == own_heads, first, jnp.where(lane == own_heads + 1, last, logs[length - 1 :]))
+    meta_ref[me] = jnp.broadcast_to(note, (8, LANES))
+    pl.semaphore_wait(barrier, n)
+    notes = [
+        send(meta_ref.at[me], meta_ref.at[me], meta_send.at[d], meta_recv.at[d], {"ctx": (me + d) % n})
+        for d in range(1, n)
+    ]
+    pending += notes
+
+    head_row = lax.broadcasted_iota(jnp.int32, (LANES, channels), 0)
+    channel = lax.broadcasted_iota(jnp.int32, (LANES, channels), 1)
+    spread = jnp.where((channel >= head_row * HEAD_DIM) & (channel < (head_row + 1) * HEAD_DIM), 1.0, 0.0)
+    tail = jnp.exp(logs_heads[:own_heads, length - 1 :] - logs_heads[:own_heads])
+    tail = tail * jnp.where(docs_row == last, 1.0, 0.0) * dt_heads
+    tail = jnp.concatenate([tail, jnp.zeros((LANES - own_heads, length), f32)], axis=0)
+    tail = exact(across(identity, tail), spread)
+    for g in range(groups):
+        part = pl.ds(g * span, span)
+        scaled = (x_ref[:, part].astype(f32) * tail[:, g * span : (g + 1) * span]).astype(jnp.bfloat16)
+        turned = b_ref[:, pl.ds(g * STATE, STATE)].astype(f32).T.astype(jnp.bfloat16)
+        state_ref[pl.ds(0, STATE), part] = jnp.dot(turned, scaled, preferred_element_type=f32).astype(jnp.bfloat16)
+    arriving = ring_hop(state_ref, STATE, STATE, state_send, state_recv, 1)
+    pending += arriving
+
+    causal = (docs_col == docs_row) & (at_row >= at_column)
+    low_lanes = lax.broadcasted_iota(jnp.int32, (length, LANES), 1) < HEAD_DIM
+    skip = exact(skip_ref[...], spread)
+    for g in range(groups):
+        state_part = pl.ds(g * STATE, STATE)
+        scores = lax.dot_general(
+            c_ref[:, state_part], b_ref[:, state_part], (((1,), (1,)), ((), ())), preferred_element_type=f32
+        )
+        scores = jnp.where(causal, scores, 0.0)
+        for pair in range(g * span // LANES, (g + 1) * span // LANES):
+            place_of = pl.ds(pair * LANES, LANES)
+            values = x_ref[:, place_of]
+            mixes = []
+            for h in (2 * pair, 2 * pair + 1):
+                gap = jnp.where(causal, logs[:, h : h + 1] - logs_heads[h : h + 1, :], 0.0)
+                mixes.append((jnp.exp(gap) * scores * dt_heads[h : h + 1, :]).astype(jnp.bfloat16))
+            none = jnp.zeros_like(values)
+            sides = jnp.concatenate([jnp.where(low_lanes, values, none), jnp.where(low_lanes, none, values)], axis=0)
+            inside = jnp.dot(jnp.concatenate(mixes, axis=1), sides, preferred_element_type=f32)
+            scan_ref[:, place_of] = inside + skip[:1, pair * LANES : (pair + 1) * LANES] * values.astype(f32)
+
+    for copy in notes:
+        copy.wait_recv()
+    running = jnp.zeros((1, LANES), f32)
+    kept = [None] * n
+    for j in reversed(range(n)):
+        line = meta_ref[j][:1]
+        earlier = jnp.where(j < me, 1.0, 0.0)
+        same = jnp.where(line[:, own_heads + 1 : own_heads + 2] == first, 1.0, 0.0)
+        kept[j] = jnp.exp(running) * same * earlier
+        running = running + jnp.where(lane < own_heads, line, 0.0) * earlier
+    reach_ref[...] = exact(jnp.concatenate(kept, axis=0), spread)
+
+    def add_state(s):
+        share_of = reach_ref[pl.ds(ring_index((place + n - s) % n, n), 1), :]
+        value = state_ref[pl.ds(slot(s) * STATE, STATE)].astype(f32) * share_of
+        if s == 1:
+            incoming_ref[...] = value
+        else:
+            incoming_ref[...] += value
+
+    for k in range(1, half + 1):
+        for copy in arriving:
+            copy.wait_recv()
+        if k < half:
+            arriving = ring_hop(state_ref, STATE, STATE, state_send, state_recv, k + 1)
+            pending += arriving
+        for s in [k, n - k] if k < half else [k]:
+            add_state(s)
+
+    since = exact(jnp.exp(logs) * jnp.where(docs_col == docs_col[:1], 1.0, 0.0), spread)
+    for g in range(groups):
+        part = pl.ds(g * span, span)
+        outer = jnp.dot(
+            c_ref[:, pl.ds(g * STATE, STATE)], incoming_ref[:, part].astype(jnp.bfloat16), preferred_element_type=f32
+        )
+        gated = scan_ref[:, part] + outer * since[:, g * span : (g + 1) * span]
+        gate_value = silu_ref[:, part].astype(f32)
+        gated = gated * silu(gate_value)
+        size = jnp.sqrt(jnp.mean(gated * gated, axis=1, keepdims=True) + EPS)
+        normed_ref[pl.ds(0, length), part] = (gated / size * norm_ref[:, part]).astype(jnp.bfloat16)
+
+    arriving = ring_hop(normed_ref, length, length, normed_send, normed_recv, 1)
+    pending += arriving
+    own_rows = pl.ds(pl.multiple_of(head * rows, 16), rows)
+    other_rows = pl.ds(pl.multiple_of((1 - head) * rows, 16), rows)
+    products = {}
+
+    def project(near):
+        value = lax.dot_general(
+            normed_ref[pl.ds(slot(near[0]) * length, len(near) * length)],
+            proj_ref[...],
+            (((1,), (1,)), ((), ())),
+            preferred_element_type=f32,
+        )
+        for i, s in enumerate(near):
+            product_ref[slot(s)] = value[i * length : (i + 1) * length]
+            product_lent_ref[slot(s)] = product_ref[slot(s), other_rows].astype(jnp.bfloat16)
+            products[s] = send(
+                product_lent_ref.at[slot(s)],
+                product_got_ref.at[slot(s)],
+                product_send.at[s],
+                product_recv.at[s],
+                sibling,
+            )
+
+    blocks = []
+
+    def deliver(s):
+        products[s].wait_recv()
+        value = product_ref[slot(s), own_rows] + product_got_ref[slot(s)].astype(f32)
+        if s == 0:
+            columns_ref[me] = value.astype(jnp.bfloat16)
+            return
+        block_ref[s] = value.astype(jnp.bfloat16)
+        owner = {"ctx": ring_index((place + n - s) % n, n)}
+        blocks.append(send(block_ref.at[s], columns_ref.at[me], block_send.at[s], block_recv.at[s], owner))
+
+    project([0])
+    ready = [0]
+    for k in range(1, half + 1):
+        for copy in arriving:
+            copy.wait_recv()
+        if k < half:
+            arriving = ring_hop(normed_ref, length, length, normed_send, normed_recv, k + 1)
+            pending += arriving
+        near = [k, n - k] if k < half else [k]
+        project(near)
+        for s in ready:
+            deliver(s)
+        ready = near
+    for s in ready:
+        deliver(s)
+    for copy in blocks:
+        copy.wait_recv()
+    pending += list(products.values()) + blocks
+    share_width = proj_ref.shape[0]
+    for j in range(n):
+        mamba_ref[:, pl.ds(j * share_width, share_width)] = columns_ref[j].astype(f32)
+
+    hidden_ref[...] = (residual_ref[...].astype(f32) + mamba_ref[...]).astype(jnp.bfloat16)
+    hidden = hidden_ref[...].astype(f32)
     scale = jnp.sqrt(jnp.mean(hidden * hidden, axis=1, keepdims=True) + EPS)
     rows_ref[pl.ds(0, rows), pl.ds(0, width)] = (hidden / scale * gain_ref[...]).astype(jnp.bfloat16)
     gate = gate_ref[...]
-    high = gate.astype(jnp.bfloat16).astype(jnp.float32)
-    lane = lax.broadcasted_iota(jnp.int32, gate.shape, 1)
+    high = gate.astype(jnp.bfloat16).astype(f32)
     rows_ref[pl.ds(0, rows), pl.ds(width, LANES)] = jnp.where(lane < LANES // 2, high, gate - high).astype(jnp.bfloat16)
 
-    pl.semaphore_wait(barrier, 3)
-
     def hop(k):
-        lo, size_up, size_down = 0, rows, rows
-        start_up, start_down = 0, 0
-        if k == half:
-            size_up, size_down, start_down = cut, rows - cut, cut
-        source_up = rows_ref.at[pl.ds(slot(k - 1) * both + start_up, size_up)]
-        target_up = rows_ref.at[pl.ds(slot(k) * both + start_up, size_up)]
-        source_down = rows_ref.at[pl.ds(slot((n - k + 1) % n) * both + start_down, size_down)]
-        target_down = rows_ref.at[pl.ds(slot(n - k) * both + start_down, size_down)]
-        return (
-            send(source_up, target_up, ag_send.at[0, k - 1], ag_recv.at[0, k - 1], after),
-            send(source_down, target_down, ag_send.at[1, k - 1], ag_recv.at[1, k - 1], before),
-        )
+        return ring_hop(rows_ref, both, rows, ag_send, ag_recv, k)
 
     def share(s):
         return send(
@@ -197,8 +403,11 @@
         block = pl.ds(first * both, count)
 
         def up(columns):
-            value = jnp.dot(
-                rows_ref[block, pl.ds(0, width)], up_ref[:, columns], preferred_element_type=jnp.float32
+            value = lax.dot_general(
+                rows_ref[block, pl.ds(0, width)],
+                up_ref[columns, :],
+                (((1,), (1,)), ((), ())),
+                preferred_element_type=jnp.float32,
             )
             value = jnp.maximum(value, 0.0)
             act_ref[pl.ds(0, count), columns] = (value * value).astype(jnp.bfloat16)
@@ -313,50 +522,115 @@
         copy.wait_recv()
     value = value + sums_ref[slot(0)].astype(jnp.float32) + sums_ref[slot(half)].astype(jnp.float32)
     out_ref[...] = value.astype(jnp.bfloat16)
-    for copy in started + list(shares.values()) + list(loans.values()) + backs:
+    for copy in pending + started + list(shares.values()) + list(loans.values()) + backs:
         copy.wait_send()
 
 
-def moe_on_ring(hidden, moe_gain, experts, gates, w_up, w_down):
+def layer_on_ring(
+    channels,
+    gate_channels,
+    bmat,
+    cmat,
+    dt,
+    rates,
+    skip,
+    norm_gain,
+    docs,
+    w_out,
+    residual,
+    moe_gain,
+    experts,
+    gates,
+    w_up,
+    w_down,
+):
     n, heads = lax.axis_size("ctx"), lax.axis_size("head")
-    rows, width = hidden.shape
+    rows, width = residual.shape
+    length, wide = channels.shape
     inner = w_up.shape[2]
+    share_width = w_out.shape[1]
     lane = jnp.arange(LANES, dtype=jnp.int32) % (LANES // 2)
     gate = jnp.sum(jnp.where(experts[:, :, None] == lane[None, None, :], gates[:, :, None], 0.0), axis=1)
+    ids = docs.astype(jnp.float32)
+    skip_row = jnp.pad(skip[None, :], ((0, 7), (0, LANES - skip.shape[0])))
     vmem = pl.BlockSpec(memory_space=pltpu.VMEM)
     anywhere = pl.BlockSpec(memory_space=pl.ANY)
-    pieces = pltpu.VMEM((n, rows, width), jnp.bfloat16)
+    bf16, f32 = jnp.bfloat16, jnp.float32
+    pieces = pltpu.VMEM((n, rows, width), bf16)
+    shares = pltpu.VMEM((n, rows, share_width), bf16)
+    ring_sem = pltpu.SemaphoreType.DMA((2, n // 2))
+    each_sem = pltpu.SemaphoreType.DMA((n,))
     return pl.pallas_call(
-        functools.partial(moe_kernel, n, heads),
-        out_shape=jax.ShapeDtypeStruct((rows, width), jnp.bfloat16),
-        in_specs=[vmem, vmem, vmem, anywhere, anywhere],
+        functools.partial(layer_kernel, n, heads),
+        out_shape=jax.ShapeDtypeStruct((rows, width), bf16),
+        in_specs=[vmem] * 14 + [anywhere] * 2,
         out_specs=vmem,
         scratch_shapes=[
-            pltpu.VMEM((n * 2 * rows, width + LANES), jnp.bfloat16),
+            pltpu.VMEM((n, 8, LANES), f32),
+            pltpu.VMEM((n, wide), f32),
+            pltpu.VMEM((n * STATE, wide), bf16),
+            pltpu.VMEM((length, wide), f32),
+            pltpu.VMEM((STATE, wide), f32),
+            pltpu.VMEM((n * length, wide), bf16),
+            pltpu.VMEM((n, length, share_width), f32),
+            shares,
+            shares,
+            shares,
+            shares,
+            pltpu.VMEM((rows, width), f32),
+            pltpu.VMEM((rows, width), bf16),
+            pltpu.VMEM((n * 2 * rows, width + LANES), bf16),
             pieces,
             pieces,
             pieces,
             pieces,
-            pltpu.VMEM((4 * rows, inner), jnp.bfloat16),
-            pltpu.VMEM((width, inner), jnp.bfloat16),
-            pltpu.VMEM((inner, width), jnp.bfloat16),
+            pltpu.VMEM((4 * rows, inner), bf16),
+            pltpu.VMEM((inner, width), bf16),
+            pltpu.VMEM((inner, width), bf16),
             pltpu.SemaphoreType.DMA((2,)),
-            pltpu.SemaphoreType.DMA((2, n // 2)),
-            pltpu.SemaphoreType.DMA((2, n // 2)),
-            pltpu.SemaphoreType.DMA((n,)),
-            pltpu.SemaphoreType.DMA((n,)),
-            pltpu.SemaphoreType.DMA((n,)),
-            pltpu.SemaphoreType.DMA((n,)),
-            pltpu.SemaphoreType.DMA((2, n // 2)),
-            pltpu.SemaphoreType.DMA((2, n // 2)),
+            each_sem,
+            each_sem,
+            ring_sem,
+            ring_sem,
+            ring_sem,
+            ring_sem,
+            each_sem,
+            each_sem,
+            each_sem,
+            each_sem,
+            ring_sem,
+            ring_sem,
+            each_sem,
+            each_sem,
+            each_sem,
+            each_sem,
+            ring_sem,
+            ring_sem,
         ],
         compiler_params=pltpu.CompilerParams(
-            collective_id=1, has_side_effects=True, vmem_limit_bytes=56 * 2**20
+            collective_id=1, has_side_effects=True, vmem_limit_bytes=58 * 2**20
         ),
         cost_estimate=pl.CostEstimate(
             flops=8 * n * rows * width * inner, bytes_accessed=4 * width * inner, transcendentals=0
         ),
-    )(hidden, moe_gain.reshape(1, width), gate, w_up, w_down)
+    )(
+        channels,
+        gate_channels,
+        bmat,
+        cmat,
+        dt.T,
+        rates[:, None],
+        skip_row,
+        norm_gain[None, :],
+        ids[:, None],
+        ids[None, :],
+        w_out.T,
+        residual,
+        moe_gain[None, :],
+        gate,
+        jnp.swapaxes(w_up, 1, 2),
+        w_down,
+    )
 
 
 def ring_fits(n, heads, rows, width):
@@ -381,6 +655,25 @@
     w_up,
     w_down,
 ):
+    if ring_fits(lax.axis_size("ctx"), lax.axis_size("head"), *residual.shape):
+        return layer_on_ring(
+            channels,
+            gate_channels,
+            bmat,
+            cmat,
+            dt,
+            rates,
+            skip,
+            norm_gain,
+            docs,
+            w_out,
+            residual,
+            moe_gain,
+            experts,
+            gates,
+            w_up,
+            w_down,
+        )
     length = channels.shape[0]
     heads = dt.shape[1]
     groups = bmat.shape[1] // STATE
@@ -438,8 +731,6 @@
         partial_value.astype(jnp.bfloat16), "head", scatter_dimension=0, tiled=True
     ).astype(jnp.float32)
     hidden = (residual.astype(jnp.float32) + mamba_out).astype(jnp.bfloat16)
-    if ring_fits(lax.axis_size("ctx"), lax.axis_size("head"), *hidden.shape):
-        return moe_on_ring(hidden, moe_gain, experts, gates, w_up, w_down)
     widened = hidden.astype(jnp.float32)
     moe_in = (
         widened / jnp.sqrt(jnp.mean(widened * widened, axis=1, keepdims=True) + EPS) * moe_gain

time: 293 us -> 154 us (0.53)
  waiting for transfers between devices: 95.5 us -> 0 us
  Pallas kernels: 76.1 us -> 144 us
  blocking collectives: 31.1 us -> 0 us
  loops' own time: 19.9 us -> 0 us
  local copies, waits for them, and re-layouts: 25.4 us -> 6.35 us
  other arithmetic: 19.3 us -> 2.73 us
  between operations: 15.4 us -> 0.01 us
  matrix products: 9.04 us -> 0 us
    all_gather x2 -> x0, waiting for transfers between devices: 94.8 us -> none  [the longest x1 53.1 us: local(): lax.all_gather(w_out, 'ctx', axis=1, tiled=True)]
    pallas_call x1, Pallas kernels: 76.1 us -> 144 us  [layer_on_ring(): pl.pallas_call(functools.partial(layer_kernel, n, heads), out_shape=jax.S...]
    another operation x2 -> x0, loops' own time: 19.9 us -> none  [the longest x1 19.8 us: entering(): return lax.fori_loop(0, size, lap, start)]
    all_gather x1 -> x0, blocking collectives: 17.9 us -> none  [entering(): everything = jax.tree.map(lambda part: lax.all_gather(part, axis), array)]
    unnamed x27 -> x1, local copies, waits for them, and re-layouts: 15.4 us -> 1.73 us
    unnamed x1 -> x0, blocking collectives: 13.1 us -> none
    select_n x9 -> x1, other arithmetic: 9.39 us -> 0.01 us  [layer_on_ring(): lane = jnp.arange(LANES, dtype=jnp.int32) % (LANES // 2)]
    dot_general x8 -> x0, matrix products: 9.04 us -> none  [the longest x1 5.36 us: local(): jnp.dot(normed_scan, lax.all_gather(w_out, 'ctx', axis=1, tiled=True), pr...]
  transfers between devices with their start and end apart: 3 -> 0, of which waited for: 2 -> 0; matrix products, arithmetic and copies ran while one was open for 9% -> 0% of each run, Pallas kernels for 0% -> 0%
where the time goes in v2:
time: 154 us; the launch traced here: 153 us
  Pallas kernels  144 us (94%)
  local copies, waits for them, and re-layouts  6.35 us (4%)
  other arithmetic  2.73 us (2%)
    pallas_call x1, Pallas kernels, layer_on_ring(): pl.pallas_call(functools.partial(layer_kernel, n, heads), out_shape=jax.S...  144 us

profile of v2, /device:TPU:0, one launch (start us, length us, event | category | flops | bytes accessed | tf_op | source)
XLA Modules:
  0.0 153.2 jit_solution(4348109500775098)
XLA Ops:
  0.0 1.2 convert_bitcast_fusion
  1.3 1.2 pad.4.skip_ref
  2.5 1.3 copy.21.rates_ref
  3.8 1.3 broadcast_in_dim.38.gain_ref
  5.1 1.5 select_reduce_fusion.gate_ref
  6.6 0.7 copy.22.docs_col_ref
  7.4 144.1 %shard_map.154 = bf16[64,2688]{1,0:T(8,128)(2,1)} custom-call(bf16[128,1024]{1,0:T(8,128)(2,1)} %x_ref.1, bf16[128,1024]{1,0:T(8,128)(2,1)} %silu_ref.1, bf16[128,256]{1,0:T(8,128)(2,1)} %b_ref.1, bf16[128,256]{1,0:T(8,128)(2,1)} %c_ref.1, f32[16,128]{1,0:T(8,128)} %bitcast.14, f32[16,1]{1,0:T(8,128)} %copy.21.rates_ref, f32[8,128]{1,0:T(8,128)} %pad.4.skip_ref, ...), custom_call_target="tpu_custom_call" | custom-call | flops 10217324544 | bytes 9977856 | tf_op jit(solution)/shard_map/pallas_call | solution.py:563
  151.5 1.7 %copy.24 = bf16[64,2688]{1,0:T(8,128)(2,1)} copy(bf16[64,2688]{1,0:T(8,128)(2,1)} %shard_map.154) | data formatting | bytes 688128
  (1 shorter events, 0.0 us)

commit v3 on v2

--- a/solution.py
+++ b/solution.py
@@ -100,7 +100,6 @@
     rates_ref,
     skip_ref,
     norm_ref,
-    docs_col_ref,
     docs_row_ref,
     proj_ref,
     residual_ref,
@@ -225,10 +224,12 @@
     lower = jnp.where(at_row >= at_column, 1.0, 0.0)
     identity = jnp.where(at_row == at_column, 1.0, 0.0)
     dt_heads = dt_ref[...]
-    slow = jnp.concatenate([-rates_ref[...] * dt_heads, jnp.zeros((LANES - own_heads, length), f32)], axis=0)
+    rates = across(identity[:own_heads, :own_heads], jnp.broadcast_to(rates_ref[...], (8, own_heads)))[:, :1]
+    slow = jnp.concatenate([-rates * dt_heads, jnp.zeros((LANES - own_heads, length), f32)], axis=0)
     logs = across(lower, slow)
     logs_heads = across(slow, lower)
-    docs_col, docs_row = docs_col_ref[...], docs_row_ref[...]
+    docs_row = docs_row_ref[...].astype(f32)
+    docs_col = across(identity, jnp.broadcast_to(docs_row, (8, length)))[:, :1]
     first, last = docs_row[:, :1], docs_row[:, length - 1 :]
     lane = lax.broadcasted_iota(jnp.int32, (1, LANES), 1)
     note = jnp.where(lane == own_heads, first, jnp.where(lane == own_heads + 1, last, logs[length - 1 :]))
@@ -257,7 +258,7 @@
 
     causal = (docs_col == docs_row) & (at_row >= at_column)
     low_lanes = lax.broadcasted_iota(jnp.int32, (length, LANES), 1) < HEAD_DIM
-    skip = exact(skip_ref[...], spread)
+    skip = exact(jnp.broadcast_to(skip_ref[...], (8, own_heads)), spread[:own_heads])
     for g in range(groups):
         state_part = pl.ds(g * STATE, STATE)
         scores = lax.dot_general(
@@ -551,8 +552,6 @@
     share_width = w_out.shape[1]
     lane = jnp.arange(LANES, dtype=jnp.int32) % (LANES // 2)
     gate = jnp.sum(jnp.where(experts[:, :, None] == lane[None, None, :], gates[:, :, None], 0.0), axis=1)
-    ids = docs.astype(jnp.float32)
-    skip_row = jnp.pad(skip[None, :], ((0, 7), (0, LANES - skip.shape[0])))
     vmem = pl.BlockSpec(memory_space=pltpu.VMEM)
     anywhere = pl.BlockSpec(memory_space=pl.ANY)
     bf16, f32 = jnp.bfloat16, jnp.float32
@@ -563,7 +562,7 @@
     return pl.pallas_call(
         functools.partial(layer_kernel, n, heads),
         out_shape=jax.ShapeDtypeStruct((rows, width), bf16),
-        in_specs=[vmem] * 14 + [anywhere] * 2,
+        in_specs=[vmem] * 13 + [anywhere] * 2,
         out_specs=vmem,
         scratch_shapes=[
             pltpu.VMEM((n, 8, LANES), f32),
@@ -619,11 +618,10 @@
         bmat,
         cmat,
         dt.T,
-        rates[:, None],
-        skip_row,
+        rates[None, :],
+        skip[None, :],
         norm_gain[None, :],
-        ids[:, None],
-        ids[None, :],
+        docs[None, :],
         w_out.T,
         residual,
         moe_gain[None, :],

time: 154 us -> 149 us (0.968)
  local copies, waits for them, and re-layouts: 6.35 us -> 3.04 us
    broadcast_in_dim x2 -> x0, local copies, waits for them, and re-layouts: 2.07 us -> none  [the longest x1 1.33 us: layer_on_ring(): rates[:, None]]
where the time goes in v3:
time: 149 us; the launch traced here: 148 us
  Pallas kernels  144 us (97%)
  local copies, waits for them, and re-layouts  3.04 us (2%)
  other arithmetic  1.49 us (1%)
    pallas_call x1, Pallas kernels, layer_on_ring(): pl.pallas_call(functools.partial(layer_kernel, n, heads), out_shape=jax.S...  144 us

profile of v3, /device:TPU:0, one launch (start us, length us, event | category | flops | bytes accessed | tf_op | source)
XLA Modules:
  0.0 148.4 jit_solution(11881613316672269310)
XLA Ops:
  0.0 1.3 broadcast_in_dim.34.gain_ref
  1.3 1.5 %select_reduce_fusion.gate_ref = f32[64,128]{1,0:T(8,128)} fusion(f32[64,6]{0,1:T(8,128)} %param.29, s32[128]{0:T(128)S(1)} %and_select_fusion, s32[64,6]{0,1:T(8,128)} %param.28), kind=kLoop, calls=%fused_computation | loop fusion | flops 139264 | bytes 36352 | tf_op jit(solution)/shard_map/reduce_sum | solution.py:554
  2.8 143.9 %shard_map.154 = bf16[64,2688]{1,0:T(8,128)(2,1)} custom-call(bf16[128,1024]{1,0:T(8,128)(2,1)} %x_ref.1, bf16[128,1024]{1,0:T(8,128)(2,1)} %silu_ref.1, bf16[128,256]{1,0:T(8,128)(2,1)} %b_ref.1, bf16[128,256]{1,0:T(8,128)(2,1)} %c_ref.1, f32[16,128]{1,0:T(8,128)} %bitcast.9, f32[1,16]{1,0:T(1,128)} %bitcast.11, f32[1,16]{1,0:T(1,128)} %bitcast.12, ...), custom_call_target="tpu_custom_call" | custom-call | flops 10217324544 | bytes 9977856 | tf_op jit(solution)/shard_map/pallas_call | solution.py:562
  146.7 1.7 %copy.20 = bf16[64,2688]{1,0:T(8,128)(2,1)} copy(bf16[64,2688]{1,0:T(8,128)(2,1)} %shard_map.154) | data formatting | bytes 688128
  (1 shorter events, 0.0 us)
